TPU v7x, 32 devices: a whole 2x2x4 slice. The times are simulated.
32 devices in a mesh: grp: 2 (over core), gz: 8 (over z, y), xy: 2 (over x).
Axes of the slice: x: 2, y: 2, z: 4, core: 2. Of those that a mesh axis runs over, the one named last changes fastest.
Arguments:
- velocity: float32 [2, 3, 8, 512, 512], P('grp', None, 'gz', 'xy'), may hold values from -6 to 6
- fringe_columns: int32 [128], replicated, may hold values from 0 to 511, as said below
Outputs:
- velocity_next: float32 [2, 3, 8, 512, 512], P('grp', None, 'gz', 'xy')
Inputs may be any that keep to these rules, and one draw needn't show every extreme that they name: `fringe_columns`: 128 consecutive precursor columns, counted modulo 512, from a start that varies; the run always passes column 511 and wraps to column 0.
All inputs are finite; a program needn't handle non-finite values.
Results may differ from a plain program's by a relative error of at most 0.0001.
Values sent between devices are 32-bit elements; how exact they have to be, the bound alone decides.
A program may use at most 64 MiB of HBM per device.

v0:
```python
import functools
import math

import jax
import jax.numpy as jnp
import ml_dtypes
import numpy as np
from jax import lax
from jax.experimental import pallas as pl
from jax.experimental.pallas import tpu as pltpu
from jax.sharding import PartitionSpec as P

STEPS = 2
CHUNKS = 4
ROWS = 8

time_step = 0.001
level_gap = 0.05
smag_coeff = 0.16
MESH = pl.DeviceIdType.MESH


def derivative_matrix(points):
    offsets = np.arange(points)
    distance = offsets[:, None] - offsets[None, :]
    safe = np.where(distance == 0, 1, distance)
    entries = 0.5 * (1.0 - 2.0 * (distance % 2)) / np.tan(np.pi * safe / points)
    return np.where(distance == 0, 0.0, entries)


def two_parts(matrix):
    single = matrix.astype(np.float32)
    high = single.astype(ml_dtypes.bfloat16)
    low = (single - high.astype(np.float32)).astype(ml_dtypes.bfloat16)
    return np.stack([high, low])


def factored(block):
    rest = block.copy()
    limit = np.abs(block).max() * 2.0**-30
    columns, rows = [], []
    while len(rows) < block.shape[1]:
        row, column = np.unravel_index(np.argmax(np.abs(rest)), rest.shape)
        if abs(rest[row, column]) < limit and len(rows) % 16 == 0:
            break
        if rest[row, column] == 0.0:
            columns.append(np.zeros_like(rest[:, 0]))
            rows.append(np.zeros_like(rest[0]))
            continue
        columns.append(rest[:, column] / rest[row, column])
        rows.append(rest[row].copy())
        rest = rest - np.outer(columns[-1], rows[-1])
    return np.stack(columns, axis=1), np.stack(rows, axis=0)


def halves(value):
    high = value.astype(jnp.bfloat16)
    return high, (value - high.astype(jnp.float32)).astype(jnp.bfloat16)


def dot(left, right):
    return jnp.dot(left, right, preferred_element_type=jnp.float32)


def dot_parts(left, right):
    return dot(left[0], right[0]) + (dot(left[0], right[1]) + dot(left[1], right[0]))


def kernel(
    sizes, in_ref, cols_ref, weight_ref, mx_ref, my_ref, gather_ref, spread_ref, out_ref,
    vel, ret, fin, vhalo, shalo, gx, gy, tend, sx, sy, sz, gsend, grecv, psend, precv,
    send_sem, recv_sem,
):
    n_gz, n_xy, width, scale = sizes
    _, rows_all, cols_all = in_ref.shape
    half = cols_all // 2
    chunk = rows_all // CHUNKS
    grp, gz, xy = lax.axis_index("grp"), lax.axis_index("gz"), lax.axis_index("xy")
    domain = lax.rem(gz, 2)
    pair = gz - domain
    level = pair + grp
    levels = n_gz
    swapped = domain != grp
    has_up = level < levels - 1
    has_down = level > 0
    is_farm = domain == 0

    def at_level(other):
        other = lax.rem(other + levels, levels)
        parity = lax.rem(other, 2)
        return (parity, other - parity + domain, xy)

    up, down = at_level(level + 1), at_level(level - 1)
    swap_to = (domain, pair + grp, xy)
    mid_to = (grp, pair + 1 - domain, xy)
    end_to = (1 - grp, gz, xy)

    def xy_to(offset):
        return (grp, gz, lax.rem(xy + offset, n_xy))

    slots = {}

    def copy(name, source, target, device):
        slot = slots.setdefault(name, len(slots))
        return pltpu.make_async_remote_copy(
            src_ref=source, dst_ref=target, send_sem=send_sem.at[slot],
            recv_sem=recv_sem.at[slot], device_id=device, device_id_type=MESH,
        )

    pending = []

    def start(condition, item):
        pending.append((condition, item))
        if condition is None:
            item.start()
        else:
            pl.when(condition)(item.start)

    def part(ref, k):
        return ref.at[:, pl.ds(k * chunk, chunk), :]

    barrier = pltpu.get_barrier_semaphore()
    for device in [up, down, mid_to, end_to] + [xy_to(o) for o in range(1, n_xy)]:
        pl.semaphore_signal(barrier, inc=1, device_id=device, device_id_type=MESH)

    @pl.when(swapped)
    def _():
        pl.semaphore_signal(barrier, inc=1, device_id=swap_to, device_id_type=MESH)
        pl.semaphore_wait(barrier, 4 + n_xy)

    @pl.when(jnp.logical_not(swapped))
    def _():
        pl.semaphore_wait(barrier, 3 + n_xy)

    def z_copies(kind, s, k):
        source, halo = (vel, vhalo) if kind == "v" else (sz, shalo)
        return (
            copy((kind, s, 0, k), part(source.at[s], k), part(halo.at[s, 0], k), up),
            copy((kind, s, 1, k), part(source.at[s], k), part(halo.at[s, 1], k), down),
        )

    def z_start(kind, s, k):
        upward, downward = z_copies(kind, s, k)
        start(has_up, upward)
        start(has_down, downward)

    def z_wait(kind, s, k):
        upward, downward = z_copies(kind, s, k)
        pl.when(has_down)(upward.wait_recv)
        pl.when(has_up)(downward.wait_recv)

    swap_in = [copy(("in", k), part(in_ref, k), part(vel.at[0], k), swap_to) for k in range(CHUNKS)]
    for k in range(CHUNKS):
        start(swapped, swap_in[k])

    @pl.when(jnp.logical_not(swapped))
    def _():
        vel[0] = in_ref[...]

    @pl.when(level == 0)
    def _():
        for s in range(STEPS):
            vhalo[s, 0] = jnp.zeros_like(vel[0])
            shalo[s, 0] = jnp.zeros_like(vel[0])

    @pl.when(level == levels - 1)
    def _():
        for s in range(STEPS):
            vhalo[s, 1] = jnp.zeros_like(vel[0])
            shalo[s, 1] = jnp.zeros_like(vel[0])

    for k in range(CHUNKS):
        pl.when(swapped)(swap_in[k].wait_recv)
        z_start("v", 0, k)

    picker = jnp.where(
        lax.broadcasted_iota(jnp.int32, (cols_all, width), 0) == cols_ref[...], 1.0, 0.0
    ).astype(jnp.bfloat16)

    def picked(field):
        high = field.astype(jnp.bfloat16)
        rest = field - high.astype(jnp.float32)
        middle = rest.astype(jnp.bfloat16)
        low = (rest - middle.astype(jnp.float32)).astype(jnp.bfloat16)
        return (dot(high, picker) + (dot(middle, picker) + dot(low, picker))) * weight_ref[...]

    def x_derived(field):
        left, right = field[:, :half], field[:, half:]
        total = dot_parts(halves(left + right), (mx_ref[0], mx_ref[1]))
        difference = dot_parts(halves(left - right), (mx_ref[2], mx_ref[3]))
        return jnp.concatenate([total + difference, total - difference], axis=1)

    def compress(index, read):
        def body(c, carry):
            gsend[index, c] = dot_parts((gather_ref[0], gather_ref[1]), halves(read(c)))
            return carry

        lax.fori_loop(0, 3, body, 0)
        for o in range(1, n_xy):
            start(None, compressed(index, o))

    def compressed(index, o):
        return copy(("g", index, o), gsend.at[index], grecv.at[index, o - 1], xy_to(o))

    def received(index, c):
        result = None
        for o in range(1, n_xy):
            term = dot_parts((spread_ref[0, o - 1], spread_ref[1, o - 1]), halves(grecv[index, o - 1, c]))
            result = term if result is None else result + term
        return result

    def g_wait(index):
        for o in range(1, n_xy):
            compressed(index, o).wait_recv()

    z_scale = 1.0 / (2.0 * level_gap)

    for s in range(STEPS):
        compress(2 * s, lambda c: vel[s, c])

        def first(c, carry):
            field = vel[s, c]
            gx[c] = x_derived(field)
            gy[c] = dot_parts((my_ref[0], my_ref[1]), halves(field))
            return carry

        lax.fori_loop(0, 3, first, 0)
        g_wait(2 * s)

        def second(c, carry):
            gy[c] = gy[c] + received(2 * s, c)
            return carry

        if n_xy > 1:
            lax.fori_loop(0, 3, second, 0)

        def pointwise(i, carry):
            rows = pl.ds(pl.multiple_of(i * ROWS, ROWS), ROWS)
            u = [vel[s, c, rows, :] for c in range(3)]
            dx = [gx[c, rows, :] for c in range(3)]
            dy = [gy[c, rows, :] for c in range(3)]
            dz = [(vhalo[s, 1, c, rows, :] - vhalo[s, 0, c, rows, :]) * z_scale for c in range(3)]
            for c in range(3):
                tend[c, rows, :] = -(u[0] * dx[c] + u[1] * dy[c] + u[2] * dz[c])
            xx, yy, zz = dx[0], dy[1], dz[2]
            xy_, xz, yz = 0.5 * (dy[0] + dx[1]), 0.5 * (dz[0] + dx[2]), 0.5 * (dz[1] + dy[2])
            total = xx * xx + yy * yy + zz * zz + 2.0 * (xy_ * xy_ + xz * xz + yz * yz)
            eddy = (2.0 * scale) * jnp.sqrt(2.0 * total)
            xy_, xz, yz = eddy * xy_, eddy * xz, eddy * yz
            sx[0, rows, :] = eddy * xx
            sx[1, rows, :] = xy_
            sx[2, rows, :] = xz
            sy[0, rows, :] = xy_
            sy[1, rows, :] = eddy * yy
            sy[2, rows, :] = yz
            sz[s, 0, rows, :] = xz
            sz[s, 1, rows, :] = yz
            sz[s, 2, rows, :] = eddy * zz
            return carry

        for k in range(CHUNKS):
            z_wait("v", s, k)
            lax.fori_loop(k * chunk // ROWS, (k + 1) * chunk // ROWS, pointwise, 0)
            z_start("s", s, k)

        compress(2 * s + 1, lambda c: sy[c])

        def third(c, carry):
            local = dot_parts((my_ref[0], my_ref[1]), halves(sy[c]))
            tend[c] = tend[c] + x_derived(sx[c]) + local
            return carry

        lax.fori_loop(0, 3, third, 0)
        g_wait(2 * s + 1)

        def fourth(c, carry):
            tend[c] = tend[c] + received(2 * s + 1, c)
            return carry

        if n_xy > 1:
            lax.fori_loop(0, 3, fourth, 0)

        last = s == STEPS - 1

        def updated(k, target):
            def body(i, carry):
                rows = pl.ds(pl.multiple_of(i * ROWS, ROWS), ROWS)
                for c in range(3):
                    along_z = (shalo[s, 1, c, rows, :] - shalo[s, 0, c, rows, :]) * z_scale
                    target[c, rows, :] = vel[s, c, rows, :] + time_step * (tend[c, rows, :] + along_z)
                return carry

            lax.fori_loop(k * chunk // ROWS, (k + 1) * chunk // ROWS, body, 0)

        def pick(k, source):
            rows = pl.ds(k * chunk, chunk)
            for c in range(3):
                psend[s, c, rows, :] = picked(source[c, rows, :])

        def blend(k, source, target):
            rows = pl.ds(k * chunk, chunk)
            for c in range(3):
                own = source[c, rows, :width] * (1.0 - weight_ref[...])
                target[c, rows, :width] = own + precv[s, c, rows, :]

        def fringe_copy(k, device):
            return copy(("f", s, k), part(psend.at[s], k), part(precv.at[s], k), device)

        if not last:
            following = vel.at[s + 1]
            for k in range(CHUNKS):
                z_wait("s", s, k)
                updated(k, following)

                @pl.when(jnp.logical_not(is_farm))
                def _():
                    pick(k, following)

                start(jnp.logical_not(is_farm), fringe_copy(k, mid_to))

                @pl.when(is_farm)
                def _():
                    fringe_copy(k, mid_to).wait_recv()
                    blend(k, following, following)

                z_start("v", s + 1, k)
        else:
            back = [copy(("out", k), part(ret, k), part(fin, k), swap_to) for k in range(CHUNKS)]
            for k in range(CHUNKS):
                z_wait("s", s, k)

                @pl.when(swapped)
                def _():
                    updated(k, ret)

                @pl.when(jnp.logical_not(swapped))
                def _():
                    updated(k, fin)

                start(swapped, back[k])
            for k in range(CHUNKS):
                pl.when(swapped)(back[k].wait_recv)

                @pl.when(grp == 1)
                def _():
                    pick(k, fin)

                start(grp == 1, fringe_copy(k, end_to))
                rows = pl.ds(k * chunk, chunk)
                out_ref[:, rows, :] = fin[:, rows, :]

                @pl.when(grp == 0)
                def _():
                    fringe_copy(k, end_to).wait_recv()
                    blend(k, fin, out_ref)

    for condition, item in pending:
        if condition is None:
            item.wait_send()
        else:
            pl.when(condition)(item.wait_send)


def per_device(velocity, fringe_columns):
    _, comps, _, rows_all, cols_all = velocity.shape
    n_xy, n_gz = lax.axis_size("xy"), lax.axis_size("gz")
    cross = rows_all * n_xy
    delta = (2.0 * math.pi / cols_all * (2.0 * math.pi / cross) * level_gap) ** (1.0 / 3.0)
    width = fringe_columns.shape[0]
    half = cols_all // 2
    along = derivative_matrix(cols_all).T
    same, other = along[:half, :half], along[half:, :half]
    mx = np.concatenate([two_parts((same + other) / 2), two_parts((same - other) / 2)])
    across = derivative_matrix(cross)
    my = two_parts(across[:rows_all, :rows_all])
    if n_xy > 1:
        spread, gather = factored(across[rows_all:, :rows_all])
    else:
        spread, gather = np.zeros((rows_all, 16)), np.zeros((16, rows_all))
    rank = gather.shape[0]
    gather = two_parts(gather)
    spread = two_parts(spread).reshape(2, -1, rows_all, rank)
    others = spread.shape[1]
    offsets = np.arange(width)
    weights = (0.5 * (1.0 + np.cos(np.pi * offsets / width))).astype(np.float32)[None]
    plane = (comps, rows_all, cols_all)
    fringe = (comps, rows_all, width)
    copies = STEPS * CHUNKS * 5 + 2 * CHUNKS + 2 * STEPS * others
    vmem = pl.BlockSpec(memory_space=pltpu.VMEM)

    def buffer(*shape):
        return pltpu.VMEM(shape, jnp.float32)

    result = pl.pallas_call(
        functools.partial(kernel, (n_gz, n_xy, width, (smag_coeff * delta) ** 2)),
        out_shape=jax.ShapeDtypeStruct(plane, jnp.float32),
        in_specs=[vmem] * 7,
        out_specs=vmem,
        scratch_shapes=[
            buffer(STEPS, *plane),
            buffer(*plane),
            buffer(*plane),
            buffer(STEPS, 2, *plane),
            buffer(STEPS, 2, *plane),
            buffer(*plane),
            buffer(*plane),
            buffer(*plane),
            buffer(*plane),
            buffer(*plane),
            buffer(STEPS, *plane),
            buffer(2 * STEPS, comps, rank, cols_all),
            buffer(2 * STEPS, others, comps, rank, cols_all),
            buffer(STEPS, *fringe),
            buffer(STEPS, *fringe),
            pltpu.SemaphoreType.DMA((copies,)),
            pltpu.SemaphoreType.DMA((copies,)),
        ],
        compiler_params=pltpu.CompilerParams(
            collective_id=0, has_side_effects=True, vmem_limit_bytes=56 * 1024 * 1024
        ),
    )(
        velocity.reshape(plane), fringe_columns.reshape(1, width), jnp.asarray(weights),
        jnp.asarray(mx), jnp.asarray(my), jnp.asarray(gather), jnp.asarray(spread),
    )
    return result.reshape(velocity.shape)


def solution(mesh):
    in_specs = (P("grp", None, "gz", "xy", None), P())
    out_specs = P("grp", None, "gz", "xy", None)
    return jax.shard_map(
        per_device, mesh=mesh, in_specs=in_specs, out_specs=out_specs, check_vma=False
    )
```

profile of v0, /device:TPU:17, one launch (start us, length us, event | category | flops | bytes accessed | tf_op | source)
XLA Modules:
  0.0 90.4 jit_solution(1152843586529873868)
XLA Ops:
  0.0 87.7 %shard_map.73 = f32[3,256,512]{2,1,0:T(8,128)} custom-call(f32[3,256,512]{2,1,0:T(8,128)} %bitcast.6, s32[1,128]{1,0:T(1,128)} %bitcast.7, f32[1,128]{1,0:T(1,128)} %constant.10.clone.weight_ref, bf16[4,256,256]{2,1,0:T(8,128)(2,1)} %constant.11.clone.mx_ref, bf16[2,256,256]{2,1,0:T(8,128)(2,1)} %constant.12.clone.my_ref, ...), custom_call_target="tpu_custom_call" | custom-call | tf_op jit(solution)/shard_map/pallas_call | solution.py:394
  87.7 2.7 %copy.10 = f32[1,3,1,256,512]{4,3,2,1,0:T(8,128)} copy(f32[1,3,1,256,512]{4,3,2,1,0:T(8,128)} %bitcast.5) | data formatting | bytes 3145728
where the time goes:
time: 91.7 us; the launch traced here: 90.4 us
  Pallas kernels  87.7 us (96%)
  local copies, waits for them, and re-layouts  2.67 us (3%)
    pallas_call x1, Pallas kernels, per_device(): pl.pallas_call(functools.partial(kernel, (n_gz, n_xy, width, (smag_coeff...  87.7 us
    unnamed x1, local copies, waits for them, and re-layouts  2.67 us

commit v1 on v0

--- a/solution.py
+++ b/solution.py
@@ -98,26 +98,41 @@
     def xy_to(offset):
         return (grp, gz, lax.rem(xy + offset, n_xy))
 
-    slots = {}
-
-    def copy(name, source, target, device):
-        slot = slots.setdefault(name, len(slots))
+    bases = {}
+
+    def copy(name, index, source, target, device):
+        slot = bases.setdefault(name, len(bases) * 3 * CHUNKS) + index
         return pltpu.make_async_remote_copy(
             src_ref=source, dst_ref=target, send_sem=send_sem.at[slot],
             recv_sem=recv_sem.at[slot], device_id=device, device_id_type=MESH,
         )
 
-    pending = []
-
-    def start(condition, item):
-        pending.append((condition, item))
+    def when(condition, action):
         if condition is None:
-            item.start()
+            action()
         else:
-            pl.when(condition)(item.start)
+            pl.when(condition)(action)
 
     def part(ref, k):
-        return ref.at[:, pl.ds(k * chunk, chunk), :]
+        return ref.at[pl.ds(k * chunk, chunk), :]
+
+    def each(body):
+        def step(c, carry):
+            body(c)
+            return carry
+
+        lax.fori_loop(0, 3, step, 0)
+
+    def flush(*waits):
+        def body(c):
+            for condition, copies in waits:
+                def wait():
+                    for item in copies(c):
+                        item.wait_send()
+
+                when(condition, wait)
+
+        each(body)
 
     barrier = pltpu.get_barrier_semaphore()
     for device in [up, down, mid_to, end_to] + [xy_to(o) for o in range(1, n_xy)]:
@@ -132,26 +147,51 @@
     def _():
         pl.semaphore_wait(barrier, 3 + n_xy)
 
-    def z_copies(kind, s, k):
+    def z_copy(kind, s, c, k, upward):
         source, halo = (vel, vhalo) if kind == "v" else (sz, shalo)
-        return (
-            copy((kind, s, 0, k), part(source.at[s], k), part(halo.at[s, 0], k), up),
-            copy((kind, s, 1, k), part(source.at[s], k), part(halo.at[s, 1], k), down),
+        side, device = (0, up) if upward else (1, down)
+        return copy(
+            (kind, s, side), c * CHUNKS + k, part(source.at[s, c], k), part(halo.at[s, side, c], k), device
         )
 
-    def z_start(kind, s, k):
-        upward, downward = z_copies(kind, s, k)
-        start(has_up, upward)
-        start(has_down, downward)
-
-    def z_wait(kind, s, k):
-        upward, downward = z_copies(kind, s, k)
-        pl.when(has_down)(upward.wait_recv)
-        pl.when(has_up)(downward.wait_recv)
-
-    swap_in = [copy(("in", k), part(in_ref, k), part(vel.at[0], k), swap_to) for k in range(CHUNKS)]
-    for k in range(CHUNKS):
-        start(swapped, swap_in[k])
+    def z_start(kind, s, c, k):
+        pl.when(has_up)(z_copy(kind, s, c, k, True).start)
+        pl.when(has_down)(z_copy(kind, s, c, k, False).start)
+
+    def z_wait(kind, s, components, k):
+        def wait(upward):
+            for c in components:
+                z_copy(kind, s, c, k, upward).wait_recv()
+
+        pl.when(has_down)(lambda: wait(True))
+        pl.when(has_up)(lambda: wait(False))
+
+    def z_flush(kind, s):
+        return [
+            (has_up, lambda c: [z_copy(kind, s, c, k, True) for k in range(CHUNKS)]),
+            (has_down, lambda c: [z_copy(kind, s, c, k, False) for k in range(CHUNKS)]),
+        ]
+
+    def swap_in(c, k):
+        return copy("in", c * CHUNKS + k, part(in_ref.at[c], k), part(vel.at[0, c], k), swap_to)
+
+    def swap_back(c, k):
+        return copy("out", c * CHUNKS + k, part(ret.at[c], k), part(fin.at[c], k), swap_to)
+
+    def fringe_copy(s, c, k):
+        device = end_to if s == STEPS - 1 else mid_to
+        return copy(("f", s), c * CHUNKS + k, part(psend.at[s, c], k), part(precv.at[s, c], k), device)
+
+    def g_copy(index, o, c):
+        return copy(("g", index, o), c, gsend.at[index, c], grecv.at[index, o - 1, c], xy_to(o))
+
+    @pl.when(swapped)
+    def _():
+        def body(c):
+            for k in range(CHUNKS):
+                swap_in(c, k).start()
+
+        each(body)
 
     @pl.when(jnp.logical_not(swapped))
     def _():
@@ -168,10 +208,6 @@
         for s in range(STEPS):
             vhalo[s, 1] = jnp.zeros_like(vel[0])
             shalo[s, 1] = jnp.zeros_like(vel[0])
-
-    for k in range(CHUNKS):
-        pl.when(swapped)(swap_in[k].wait_recv)
-        z_start("v", 0, k)
 
     picker = jnp.where(
         lax.broadcasted_iota(jnp.int32, (cols_all, width), 0) == cols_ref[...], 1.0, 0.0
@@ -190,49 +226,47 @@
         difference = dot_parts(halves(left - right), (mx_ref[2], mx_ref[3]))
         return jnp.concatenate([total + difference, total - difference], axis=1)
 
-    def compress(index, read):
-        def body(c, carry):
-            gsend[index, c] = dot_parts((gather_ref[0], gather_ref[1]), halves(read(c)))
-            return carry
-
-        lax.fori_loop(0, 3, body, 0)
+    def compress(index, c, field):
+        gsend[index, c] = dot_parts((gather_ref[0], gather_ref[1]), field)
         for o in range(1, n_xy):
-            start(None, compressed(index, o))
-
-    def compressed(index, o):
-        return copy(("g", index, o), gsend.at[index], grecv.at[index, o - 1], xy_to(o))
+            g_copy(index, o, c).start()
 
     def received(index, c):
         result = None
         for o in range(1, n_xy):
+            g_copy(index, o, c).wait_recv()
             term = dot_parts((spread_ref[0, o - 1], spread_ref[1, o - 1]), halves(grecv[index, o - 1, c]))
             result = term if result is None else result + term
         return result
 
-    def g_wait(index):
-        for o in range(1, n_xy):
-            compressed(index, o).wait_recv()
+    def g_flush(index):
+        return (None, lambda c: [g_copy(index, o, c) for o in range(1, n_xy)])
+
+    def derive(s, c):
+        field = vel[s, c]
+        parts = halves(field)
+        compress(2 * s, c, parts)
+        gy[c] = dot_parts((my_ref[0], my_ref[1]), parts)
+        gx[c] = x_derived(field)
 
     z_scale = 1.0 / (2.0 * level_gap)
 
+    def arrive(c):
+        for k in range(CHUNKS):
+            pl.when(swapped)(swap_in(c, k).wait_recv)
+            z_start("v", 0, c, k)
+        derive(0, c)
+
+    each(arrive)
+
     for s in range(STEPS):
-        compress(2 * s, lambda c: vel[s, c])
-
-        def first(c, carry):
-            field = vel[s, c]
-            gx[c] = x_derived(field)
-            gy[c] = dot_parts((my_ref[0], my_ref[1]), halves(field))
-            return carry
-
-        lax.fori_loop(0, 3, first, 0)
-        g_wait(2 * s)
-
-        def second(c, carry):
-            gy[c] = gy[c] + received(2 * s, c)
-            return carry
-
-        if n_xy > 1:
-            lax.fori_loop(0, 3, second, 0)
+        last = s == STEPS - 1
+
+        def second(c):
+            if n_xy > 1:
+                gy[c] = gy[c] + received(2 * s, c)
+
+        each(second)
 
         def pointwise(i, carry):
             rows = pl.ds(pl.multiple_of(i * ROWS, ROWS), ROWS)
@@ -259,106 +293,102 @@
             return carry
 
         for k in range(CHUNKS):
-            z_wait("v", s, k)
+            z_wait("v", s, range(3), k)
             lax.fori_loop(k * chunk // ROWS, (k + 1) * chunk // ROWS, pointwise, 0)
-            z_start("s", s, k)
-
-        compress(2 * s + 1, lambda c: sy[c])
-
-        def third(c, carry):
-            local = dot_parts((my_ref[0], my_ref[1]), halves(sy[c]))
-            tend[c] = tend[c] + x_derived(sx[c]) + local
-            return carry
-
-        lax.fori_loop(0, 3, third, 0)
-        g_wait(2 * s + 1)
-
-        def fourth(c, carry):
-            tend[c] = tend[c] + received(2 * s + 1, c)
-            return carry
-
-        if n_xy > 1:
-            lax.fori_loop(0, 3, fourth, 0)
-
-        last = s == STEPS - 1
-
-        def updated(k, target):
-            def body(i, carry):
-                rows = pl.ds(pl.multiple_of(i * ROWS, ROWS), ROWS)
-                for c in range(3):
-                    along_z = (shalo[s, 1, c, rows, :] - shalo[s, 0, c, rows, :]) * z_scale
-                    target[c, rows, :] = vel[s, c, rows, :] + time_step * (tend[c, rows, :] + along_z)
-                return carry
-
-            lax.fori_loop(k * chunk // ROWS, (k + 1) * chunk // ROWS, body, 0)
-
-        def pick(k, source):
+            z_start("s", s, 0, k)
+        for c in (1, 2):
+            for k in range(CHUNKS):
+                z_start("s", s, c, k)
+
+        def third(c):
+            parts = halves(sy[c])
+            compress(2 * s + 1, c, parts)
+            tend[c] = tend[c] + (x_derived(sx[c]) + dot_parts((my_ref[0], my_ref[1]), parts))
+
+        each(third)
+
+        def fourth(c):
+            if n_xy > 1:
+                tend[c] = tend[c] + received(2 * s + 1, c)
+
+        each(fourth)
+        flush(*z_flush("v", s), g_flush(2 * s), g_flush(2 * s + 1))
+
+        def update(c, k, target):
+            z_wait("s", s, [c], k)
             rows = pl.ds(k * chunk, chunk)
-            for c in range(3):
-                psend[s, c, rows, :] = picked(source[c, rows, :])
-
-        def blend(k, source, target):
+            along_z = (shalo[s, 1, c, rows, :] - shalo[s, 0, c, rows, :]) * z_scale
+            target[c, rows, :] = vel[s, c, rows, :] + time_step * (tend[c, rows, :] + along_z)
+
+        def pick(c, k, source):
             rows = pl.ds(k * chunk, chunk)
-            for c in range(3):
-                own = source[c, rows, :width] * (1.0 - weight_ref[...])
-                target[c, rows, :width] = own + precv[s, c, rows, :]
-
-        def fringe_copy(k, device):
-            return copy(("f", s, k), part(psend.at[s], k), part(precv.at[s], k), device)
+            psend[s, c, rows, :] = picked(source[c, rows, :])
+            fringe_copy(s, c, k).start()
+
+        def blend(c, k, source, target):
+            fringe_copy(s, c, k).wait_recv()
+            rows = pl.ds(k * chunk, chunk)
+            own = source[c, rows, :width] * (1.0 - weight_ref[...])
+            target[c, rows, :width] = own + precv[s, c, rows, :]
 
         if not last:
             following = vel.at[s + 1]
-            for k in range(CHUNKS):
-                z_wait("s", s, k)
-                updated(k, following)
-
-                @pl.when(jnp.logical_not(is_farm))
-                def _():
-                    pick(k, following)
-
-                start(jnp.logical_not(is_farm), fringe_copy(k, mid_to))
+
+            def advance(c):
+                for k in range(CHUNKS):
+                    update(c, k, following)
+
+                    @pl.when(jnp.logical_not(is_farm))
+                    def _():
+                        pick(c, k, following)
+                        z_start("v", s + 1, c, k)
 
                 @pl.when(is_farm)
                 def _():
-                    fringe_copy(k, mid_to).wait_recv()
-                    blend(k, following, following)
-
-                z_start("v", s + 1, k)
+                    for k in range(CHUNKS):
+                        blend(c, k, following, following)
+                        z_start("v", s + 1, c, k)
+
+                derive(s + 1, c)
+
+            each(advance)
+            flush(*z_flush("s", s))
         else:
-            back = [copy(("out", k), part(ret, k), part(fin, k), swap_to) for k in range(CHUNKS)]
-            for k in range(CHUNKS):
-                z_wait("s", s, k)
-
-                @pl.when(swapped)
-                def _():
-                    updated(k, ret)
-
-                @pl.when(jnp.logical_not(swapped))
-                def _():
-                    updated(k, fin)
-
-                start(swapped, back[k])
-            for k in range(CHUNKS):
-                pl.when(swapped)(back[k].wait_recv)
-
-                @pl.when(grp == 1)
-                def _():
-                    pick(k, fin)
-
-                start(grp == 1, fringe_copy(k, end_to))
-                rows = pl.ds(k * chunk, chunk)
-                out_ref[:, rows, :] = fin[:, rows, :]
+            def finish(c):
+                for k in range(CHUNKS):
+                    pl.when(swapped)(swap_back(c, k).wait_recv)
+                    pl.when(grp == 1)(lambda: pick(c, k, fin))
+                    rows = pl.ds(k * chunk, chunk)
+                    out_ref[c, rows, :] = fin[c, rows, :]
 
                 @pl.when(grp == 0)
                 def _():
-                    fringe_copy(k, end_to).wait_recv()
-                    blend(k, fin, out_ref)
-
-    for condition, item in pending:
-        if condition is None:
-            item.wait_send()
-        else:
-            pl.when(condition)(item.wait_send)
+                    for k in range(CHUNKS):
+                        blend(c, k, fin, out_ref)
+
+            def advance(c):
+                for k in range(CHUNKS):
+                    @pl.when(swapped)
+                    def _():
+                        update(c, k, ret)
+                        swap_back(c, k).start()
+
+                    pl.when(jnp.logical_not(swapped))(lambda: update(c, k, fin))
+
+                pl.when(c > 0)(lambda: finish(c - 1))
+
+            each(advance)
+            finish(2)
+            flush(
+                *z_flush("s", s),
+                (swapped, lambda c: [swap_in(c, k) for k in range(CHUNKS)]),
+                (swapped, lambda c: [swap_back(c, k) for k in range(CHUNKS)]),
+                (grp == 1, lambda c: [fringe_copy(s, c, k) for k in range(CHUNKS)]),
+                *[
+                    (jnp.logical_not(is_farm), lambda c, t=t: [fringe_copy(t, c, k) for k in range(CHUNKS)])
+                    for t in range(STEPS - 1)
+                ],
+            )
 
 
 def per_device(velocity, fringe_columns):
@@ -385,7 +415,7 @@
     weights = (0.5 * (1.0 + np.cos(np.pi * offsets / width))).astype(np.float32)[None]
     plane = (comps, rows_all, cols_all)
     fringe = (comps, rows_all, width)
-    copies = STEPS * CHUNKS * 5 + 2 * CHUNKS + 2 * STEPS * others
+    copies = 3 * CHUNKS * (STEPS * 5 + 2 + 2 * STEPS * others)
     vmem = pl.BlockSpec(memory_space=pltpu.VMEM)
 
     def buffer(*shape):

time: 91.7 us -> 94.5 us (1.031)
  Pallas kernels: 87.7 us -> 90.4 us
    pallas_call x1, Pallas kernels: 87.7 us -> 90.4 us  [per_device(): pl.pallas_call(functools.partial(kernel, (n_gz, n_xy, width, (smag_coeff...]
where the time goes in v1:
time: 94.5 us; the launch traced here: 93.1 us
  Pallas kernels  90.4 us (96%)
  local copies, waits for them, and re-layouts  2.67 us (3%)
    pallas_call x1, Pallas kernels, per_device(): pl.pallas_call(functools.partial(kernel, (n_gz, n_xy, width, (smag_coeff...  90.4 us
    unnamed x1, local copies, waits for them, and re-layouts  2.67 us

profile of v1, /device:TPU:17, one launch (start us, length us, event | category | flops | bytes accessed | tf_op | source)
XLA Modules:
  0.0 93.1 jit_solution(5310080872475442573)
XLA Ops:
  0.0 90.4 %shard_map.73 = f32[3,256,512]{2,1,0:T(8,128)} custom-call(f32[3,256,512]{2,1,0:T(8,128)} %bitcast.6, s32[1,128]{1,0:T(1,128)} %bitcast.7, f32[1,128]{1,0:T(1,128)} %constant.10.clone.weight_ref, bf16[4,256,256]{2,1,0:T(8,128)(2,1)} %constant.11.clone.mx_ref, bf16[2,256,256]{2,1,0:T(8,128)(2,1)} %constant.12.clone.my_ref, ...), custom_call_target="tpu_custom_call" | custom-call | tf_op jit(solution)/shard_map/pallas_call | solution.py:424
  90.4 2.7 %copy.10 = f32[1,3,1,256,512]{4,3,2,1,0:T(8,128)} copy(f32[1,3,1,256,512]{4,3,2,1,0:T(8,128)} %bitcast.5) | data formatting | bytes 3145728

commit v2 on v1

--- a/solution.py
+++ b/solution.py
@@ -13,6 +13,7 @@
 STEPS = 2
 CHUNKS = 4
 ROWS = 8
+BLOCK = 256
 
 time_step = 0.001
 level_gap = 0.05
@@ -62,12 +63,8 @@
     return jnp.dot(left, right, preferred_element_type=jnp.float32)
 
 
-def dot_parts(left, right):
-    return dot(left[0], right[0]) + (dot(left[0], right[1]) + dot(left[1], right[0]))
-
-
 def kernel(
-    sizes, in_ref, cols_ref, weight_ref, mx_ref, my_ref, gather_ref, spread_ref, out_ref,
+    sizes, in_ref, cols_ref, weight_ref, mx_ref, my_ref, spread_ref, out_ref,
     vel, ret, fin, vhalo, shalo, gx, gy, tend, sx, sy, sz, gsend, grecv, psend, precv,
     send_sem, recv_sem,
 ):
@@ -218,24 +215,34 @@
         rest = field - high.astype(jnp.float32)
         middle = rest.astype(jnp.bfloat16)
         low = (rest - middle.astype(jnp.float32)).astype(jnp.bfloat16)
-        return (dot(high, picker) + (dot(middle, picker) + dot(low, picker))) * weight_ref[...]
+        wide = dot(jnp.concatenate([high, middle, low], axis=0), picker)
+        return (wide[:chunk] + (wide[chunk : 2 * chunk] + wide[2 * chunk :])) * weight_ref[...]
 
     def x_derived(field):
         left, right = field[:, :half], field[:, half:]
-        total = dot_parts(halves(left + right), (mx_ref[0], mx_ref[1]))
-        difference = dot_parts(halves(left - right), (mx_ref[2], mx_ref[3]))
-        return jnp.concatenate([total + difference, total - difference], axis=1)
-
-    def compress(index, c, field):
-        gsend[index, c] = dot_parts((gather_ref[0], gather_ref[1]), field)
+        both = []
+        for at, value in ((0, left + right), (2, left - right)):
+            high, low = halves(value)
+            wide = dot(jnp.concatenate([high, low], axis=0), mx_ref[at])
+            both.append(wide[:rows_all] + (wide[rows_all:] + dot(high, mx_ref[at + 1])))
+        return jnp.concatenate([both[0] + both[1], both[0] - both[1]], axis=1)
+
+    def y_derived(index, c, field):
+        high, low = halves(field)
+        lines = my_ref.shape[0] // 2
+        wide = dot(my_ref[...], high)
+        total = wide[:lines] + (wide[lines:] + dot(my_ref[:lines, :], low))
+        gsend[index, c] = total[rows_all:]
         for o in range(1, n_xy):
             g_copy(index, o, c).start()
+        return total[:rows_all]
 
     def received(index, c):
         result = None
         for o in range(1, n_xy):
             g_copy(index, o, c).wait_recv()
-            term = dot_parts((spread_ref[0, o - 1], spread_ref[1, o - 1]), halves(grecv[index, o - 1, c]))
+            high, low = halves(grecv[index, o - 1, c])
+            term = dot(spread_ref[o - 1], jnp.concatenate([high, high, low], axis=0))
             result = term if result is None else result + term
         return result
 
@@ -244,9 +251,7 @@
 
     def derive(s, c):
         field = vel[s, c]
-        parts = halves(field)
-        compress(2 * s, c, parts)
-        gy[c] = dot_parts((my_ref[0], my_ref[1]), parts)
+        gy[c] = y_derived(2 * s, c, field)
         gx[c] = x_derived(field)
 
     z_scale = 1.0 / (2.0 * level_gap)
@@ -269,28 +274,31 @@
         each(second)
 
         def pointwise(i, carry):
-            rows = pl.ds(pl.multiple_of(i * ROWS, ROWS), ROWS)
-            u = [vel[s, c, rows, :] for c in range(3)]
-            dx = [gx[c, rows, :] for c in range(3)]
-            dy = [gy[c, rows, :] for c in range(3)]
-            dz = [(vhalo[s, 1, c, rows, :] - vhalo[s, 0, c, rows, :]) * z_scale for c in range(3)]
+            for first in range(0, cols_all, BLOCK):
+                block(pl.ds(pl.multiple_of(i * ROWS, ROWS), ROWS), pl.ds(first, BLOCK))
+            return carry
+
+        def block(rows, lanes):
+            u = [vel[s, c, rows, lanes] for c in range(3)]
+            dx = [gx[c, rows, lanes] for c in range(3)]
+            dy = [gy[c, rows, lanes] for c in range(3)]
+            dz = [(vhalo[s, 1, c, rows, lanes] - vhalo[s, 0, c, rows, lanes]) * z_scale for c in range(3)]
             for c in range(3):
-                tend[c, rows, :] = -(u[0] * dx[c] + u[1] * dy[c] + u[2] * dz[c])
+                tend[c, rows, lanes] = -(u[0] * dx[c] + u[1] * dy[c] + u[2] * dz[c])
             xx, yy, zz = dx[0], dy[1], dz[2]
             xy_, xz, yz = 0.5 * (dy[0] + dx[1]), 0.5 * (dz[0] + dx[2]), 0.5 * (dz[1] + dy[2])
             total = xx * xx + yy * yy + zz * zz + 2.0 * (xy_ * xy_ + xz * xz + yz * yz)
             eddy = (2.0 * scale) * jnp.sqrt(2.0 * total)
             xy_, xz, yz = eddy * xy_, eddy * xz, eddy * yz
-            sx[0, rows, :] = eddy * xx
-            sx[1, rows, :] = xy_
-            sx[2, rows, :] = xz
-            sy[0, rows, :] = xy_
-            sy[1, rows, :] = eddy * yy
-            sy[2, rows, :] = yz
-            sz[s, 0, rows, :] = xz
-            sz[s, 1, rows, :] = yz
-            sz[s, 2, rows, :] = eddy * zz
-            return carry
+            sx[0, rows, lanes] = eddy * xx
+            sx[1, rows, lanes] = xy_
+            sx[2, rows, lanes] = xz
+            sy[0, rows, lanes] = xy_
+            sy[1, rows, lanes] = eddy * yy
+            sy[2, rows, lanes] = yz
+            sz[s, 0, rows, lanes] = xz
+            sz[s, 1, rows, lanes] = yz
+            sz[s, 2, rows, lanes] = eddy * zz
 
         for k in range(CHUNKS):
             z_wait("v", s, range(3), k)
@@ -301,9 +309,8 @@
                 z_start("s", s, c, k)
 
         def third(c):
-            parts = halves(sy[c])
-            compress(2 * s + 1, c, parts)
-            tend[c] = tend[c] + (x_derived(sx[c]) + dot_parts((my_ref[0], my_ref[1]), parts))
+            tend[c] = tend[c] + y_derived(2 * s + 1, c, sy[c])
+            tend[c] = tend[c] + x_derived(sx[c])
 
         each(third)
 
@@ -402,15 +409,15 @@
     same, other = along[:half, :half], along[half:, :half]
     mx = np.concatenate([two_parts((same + other) / 2), two_parts((same - other) / 2)])
     across = derivative_matrix(cross)
-    my = two_parts(across[:rows_all, :rows_all])
     if n_xy > 1:
         spread, gather = factored(across[rows_all:, :rows_all])
     else:
         spread, gather = np.zeros((rows_all, 16)), np.zeros((16, rows_all))
     rank = gather.shape[0]
-    gather = two_parts(gather)
-    spread = two_parts(spread).reshape(2, -1, rows_all, rank)
-    others = spread.shape[1]
+    my = np.concatenate(two_parts(np.concatenate([across[:rows_all, :rows_all], gather])))
+    high, low = two_parts(spread)
+    spread = np.concatenate([high, low, high], axis=1).reshape(-1, rows_all, 3 * rank)
+    others = spread.shape[0]
     offsets = np.arange(width)
     weights = (0.5 * (1.0 + np.cos(np.pi * offsets / width))).astype(np.float32)[None]
     plane = (comps, rows_all, cols_all)
@@ -424,7 +431,7 @@
     result = pl.pallas_call(
         functools.partial(kernel, (n_gz, n_xy, width, (smag_coeff * delta) ** 2)),
         out_shape=jax.ShapeDtypeStruct(plane, jnp.float32),
-        in_specs=[vmem] * 7,
+        in_specs=[vmem] * 6,
         out_specs=vmem,
         scratch_shapes=[
             buffer(STEPS, *plane),
@@ -450,7 +457,7 @@
         ),
     )(
         velocity.reshape(plane), fringe_columns.reshape(1, width), jnp.asarray(weights),
-        jnp.asarray(mx), jnp.asarray(my), jnp.asarray(gather), jnp.asarray(spread),
+        jnp.asarray(mx), jnp.asarray(my), jnp.asarray(spread),
     )
     return result.reshape(velocity.shape)
 

time: 94.5 us -> 94.4 us (level)
  no operation moved by 1% of the time
where the time goes in v2:
time: 94.4 us; the launch traced here: 93 us
  Pallas kernels  90.3 us (96%)
  local copies, waits for them, and re-layouts  2.67 us (3%)
    pallas_call x1, Pallas kernels, per_device(): pl.pallas_call(functools.partial(kernel, (n_gz, n_xy, width, (smag_coeff...  90.3 us
    unnamed x1, local copies, waits for them, and re-layouts  2.67 us

profile of v2, /device:TPU:17, one launch (start us, length us, event | category | flops | bytes accessed | tf_op | source)
XLA Modules:
  0.0 93.0 jit_solution(13723956782286370385)
XLA Ops:
  0.0 90.3 %shard_map.64 = f32[3,256,512]{2,1,0:T(8,128)} custom-call(f32[3,256,512]{2,1,0:T(8,128)} %bitcast.6, s32[1,128]{1,0:T(1,128)} %bitcast.7, f32[1,128]{1,0:T(1,128)} %constant.8.clone.weight_ref, bf16[4,256,256]{2,1,0:T(8,128)(2,1)} %constant.9.clone.mx_ref, bf16[576,256]{1,0:T(8,128)(2,1)} %constant.10.clone.my_ref, ...), custom_call_target="tpu_custom_call" | custom-call | tf_op jit(solution)/shard_map/pallas_call | solution.py:431
  90.4 2.7 %copy.9 = f32[1,3,1,256,512]{4,3,2,1,0:T(8,128)} copy(f32[1,3,1,256,512]{4,3,2,1,0:T(8,128)} %bitcast.5) | data formatting | bytes 3145728

commit v3 on v2

--- a/solution.py
+++ b/solution.py
@@ -11,7 +11,7 @@
 from jax.sharding import PartitionSpec as P
 
 STEPS = 2
-CHUNKS = 4
+CHUNKS = 2
 ROWS = 8
 BLOCK = 256
 
@@ -111,25 +111,31 @@
             pl.when(condition)(action)
 
     def part(ref, k):
-        return ref.at[pl.ds(k * chunk, chunk), :]
+        return ref.at[pl.ds(k[0] * chunk, k[1] * chunk), :]
+
+    whole = [(0, CHUNKS)]
+    split = [(k, 1) for k in range(CHUNKS)]
+
+    def pieces(kind, s, c):
+        if kind == "v":
+            return split if c == 2 else whole
+        return split if c == 0 or (c == 2 and s == STEPS - 1) else whole
+
+    def ending(kind, s, c, k):
+        return [piece for piece in pieces(kind, s, c) if piece[0] + piece[1] - 1 == k]
 
     def each(body):
-        def step(c, carry):
+        for c in range(3):
             body(c)
-            return carry
-
-        lax.fori_loop(0, 3, step, 0)
 
     def flush(*waits):
-        def body(c):
-            for condition, copies in waits:
-                def wait():
+        for condition, copies in waits:
+            def wait():
+                for c in range(3):
                     for item in copies(c):
                         item.wait_send()
 
-                when(condition, wait)
-
-        each(body)
+            when(condition, wait)
 
     barrier = pltpu.get_barrier_semaphore()
     for device in [up, down, mid_to, end_to] + [xy_to(o) for o in range(1, n_xy)]:
@@ -148,47 +154,41 @@
         source, halo = (vel, vhalo) if kind == "v" else (sz, shalo)
         side, device = (0, up) if upward else (1, down)
         return copy(
-            (kind, s, side), c * CHUNKS + k, part(source.at[s, c], k), part(halo.at[s, side, c], k), device
+            (kind, s, side), c * CHUNKS + k[0], part(source.at[s, c], k), part(halo.at[s, side, c], k), device
         )
 
     def z_start(kind, s, c, k):
         pl.when(has_up)(z_copy(kind, s, c, k, True).start)
         pl.when(has_down)(z_copy(kind, s, c, k, False).start)
 
-    def z_wait(kind, s, components, k):
-        def wait(upward):
-            for c in components:
-                z_copy(kind, s, c, k, upward).wait_recv()
-
-        pl.when(has_down)(lambda: wait(True))
-        pl.when(has_up)(lambda: wait(False))
+    def z_wait(kind, s, c, k):
+        pl.when(has_down)(z_copy(kind, s, c, k, True).wait_recv)
+        pl.when(has_up)(z_copy(kind, s, c, k, False).wait_recv)
 
     def z_flush(kind, s):
         return [
-            (has_up, lambda c: [z_copy(kind, s, c, k, True) for k in range(CHUNKS)]),
-            (has_down, lambda c: [z_copy(kind, s, c, k, False) for k in range(CHUNKS)]),
+            (has_up, lambda c: [z_copy(kind, s, c, k, True) for k in pieces(kind, s, c)]),
+            (has_down, lambda c: [z_copy(kind, s, c, k, False) for k in pieces(kind, s, c)]),
         ]
 
     def swap_in(c, k):
-        return copy("in", c * CHUNKS + k, part(in_ref.at[c], k), part(vel.at[0, c], k), swap_to)
+        return copy("in", c * CHUNKS + k[0], part(in_ref.at[c], k), part(vel.at[0, c], k), swap_to)
 
     def swap_back(c, k):
-        return copy("out", c * CHUNKS + k, part(ret.at[c], k), part(fin.at[c], k), swap_to)
+        return copy("out", c * CHUNKS + k[0], part(ret.at[c], k), part(fin.at[c], k), swap_to)
 
     def fringe_copy(s, c, k):
         device = end_to if s == STEPS - 1 else mid_to
-        return copy(("f", s), c * CHUNKS + k, part(psend.at[s, c], k), part(precv.at[s, c], k), device)
+        return copy(("f", s), c * CHUNKS + k[0], part(psend.at[s, c], k), part(precv.at[s, c], k), device)
 
     def g_copy(index, o, c):
         return copy(("g", index, o), c, gsend.at[index, c], grecv.at[index, o - 1, c], xy_to(o))
 
     @pl.when(swapped)
     def _():
-        def body(c):
-            for k in range(CHUNKS):
+        for c in range(3):
+            for k in pieces("v", 0, c):
                 swap_in(c, k).start()
-
-        each(body)
 
     @pl.when(jnp.logical_not(swapped))
     def _():
@@ -216,7 +216,8 @@
         middle = rest.astype(jnp.bfloat16)
         low = (rest - middle.astype(jnp.float32)).astype(jnp.bfloat16)
         wide = dot(jnp.concatenate([high, middle, low], axis=0), picker)
-        return (wide[:chunk] + (wide[chunk : 2 * chunk] + wide[2 * chunk :])) * weight_ref[...]
+        lines = field.shape[0]
+        return (wide[:lines] + (wide[lines : 2 * lines] + wide[2 * lines :])) * weight_ref[...]
 
     def x_derived(field):
         left, right = field[:, :half], field[:, half:]
@@ -257,7 +258,7 @@
     z_scale = 1.0 / (2.0 * level_gap)
 
     def arrive(c):
-        for k in range(CHUNKS):
+        for k in pieces("v", 0, c):
             pl.when(swapped)(swap_in(c, k).wait_recv)
             z_start("v", 0, c, k)
         derive(0, c)
@@ -301,12 +302,18 @@
             sz[s, 2, rows, lanes] = eddy * zz
 
         for k in range(CHUNKS):
-            z_wait("v", s, range(3), k)
+            for c in range(3):
+                for piece in pieces("v", s, c):
+                    if piece[0] == k:
+                        z_wait("v", s, c, piece)
             lax.fori_loop(k * chunk // ROWS, (k + 1) * chunk // ROWS, pointwise, 0)
-            z_start("s", s, 0, k)
+            for c in range(3):
+                for piece in ending("s", s, c, k):
+                    if c == 0:
+                        z_start("s", s, c, piece)
         for c in (1, 2):
-            for k in range(CHUNKS):
-                z_start("s", s, c, k)
+            for piece in pieces("s", s, c):
+                z_start("s", s, c, piece)
 
         def third(c):
             tend[c] = tend[c] + y_derived(2 * s + 1, c, sy[c])
@@ -321,20 +328,22 @@
         each(fourth)
         flush(*z_flush("v", s), g_flush(2 * s), g_flush(2 * s + 1))
 
+        def rows_of(k):
+            return pl.ds(k[0] * chunk, k[1] * chunk)
+
         def update(c, k, target):
-            z_wait("s", s, [c], k)
-            rows = pl.ds(k * chunk, chunk)
+            z_wait("s", s, c, k)
+            rows = rows_of(k)
             along_z = (shalo[s, 1, c, rows, :] - shalo[s, 0, c, rows, :]) * z_scale
             target[c, rows, :] = vel[s, c, rows, :] + time_step * (tend[c, rows, :] + along_z)
 
         def pick(c, k, source):
-            rows = pl.ds(k * chunk, chunk)
-            psend[s, c, rows, :] = picked(source[c, rows, :])
+            psend[s, c, rows_of(k), :] = picked(source[c, rows_of(k), :])
             fringe_copy(s, c, k).start()
 
         def blend(c, k, source, target):
             fringe_copy(s, c, k).wait_recv()
-            rows = pl.ds(k * chunk, chunk)
+            rows = rows_of(k)
             own = source[c, rows, :width] * (1.0 - weight_ref[...])
             target[c, rows, :width] = own + precv[s, c, rows, :]
 
@@ -342,17 +351,18 @@
             following = vel.at[s + 1]
 
             def advance(c):
-                for k in range(CHUNKS):
+                for k in pieces("s", s, c):
                     update(c, k, following)
 
-                    @pl.when(jnp.logical_not(is_farm))
-                    def _():
+                @pl.when(jnp.logical_not(is_farm))
+                def _():
+                    for k in pieces("v", s + 1, c):
                         pick(c, k, following)
                         z_start("v", s + 1, c, k)
 
                 @pl.when(is_farm)
                 def _():
-                    for k in range(CHUNKS):
+                    for k in pieces("v", s + 1, c):
                         blend(c, k, following, following)
                         z_start("v", s + 1, c, k)
 
@@ -362,19 +372,18 @@
             flush(*z_flush("s", s))
         else:
             def finish(c):
-                for k in range(CHUNKS):
+                for k in pieces("s", s, c):
                     pl.when(swapped)(swap_back(c, k).wait_recv)
                     pl.when(grp == 1)(lambda: pick(c, k, fin))
-                    rows = pl.ds(k * chunk, chunk)
-                    out_ref[c, rows, :] = fin[c, rows, :]
+                    out_ref[c, rows_of(k), :] = fin[c, rows_of(k), :]
 
                 @pl.when(grp == 0)
                 def _():
-                    for k in range(CHUNKS):
+                    for k in pieces("s", s, c):
                         blend(c, k, fin, out_ref)
 
             def advance(c):
-                for k in range(CHUNKS):
+                for k in pieces("s", s, c):
                     @pl.when(swapped)
                     def _():
                         update(c, k, ret)
@@ -382,17 +391,21 @@
 
                     pl.when(jnp.logical_not(swapped))(lambda: update(c, k, fin))
 
-                pl.when(c > 0)(lambda: finish(c - 1))
+                if c > 0:
+                    finish(c - 1)
 
             each(advance)
             finish(2)
             flush(
                 *z_flush("s", s),
-                (swapped, lambda c: [swap_in(c, k) for k in range(CHUNKS)]),
-                (swapped, lambda c: [swap_back(c, k) for k in range(CHUNKS)]),
-                (grp == 1, lambda c: [fringe_copy(s, c, k) for k in range(CHUNKS)]),
+                (swapped, lambda c: [swap_in(c, k) for k in pieces("v", 0, c)]),
+                (swapped, lambda c: [swap_back(c, k) for k in pieces("s", s, c)]),
+                (grp == 1, lambda c: [fringe_copy(s, c, k) for k in pieces("s", s, c)]),
                 *[
-                    (jnp.logical_not(is_farm), lambda c, t=t: [fringe_copy(t, c, k) for k in range(CHUNKS)])
+                    (
+                        jnp.logical_not(is_farm),
+                        lambda c, t=t: [fringe_copy(t, c, k) for k in pieces("v", t + 1, c)],
+                    )
                     for t in range(STEPS - 1)
                 ],
             )

time: 94.4 us -> 98.9 us (1.048); the launches traced: 93 us -> 98.7 us
  Pallas kernels: 90.3 us -> 96 us
    pallas_call x1, Pallas kernels: 90.3 us -> 96 us  [per_device(): pl.pallas_call(functools.partial(kernel, (n_gz, n_xy, width, (smag_coeff...]
where the time goes in v3:
time: 98.9 us; the launch traced here: 98.7 us
  Pallas kernels  96 us (97%)
  local copies, waits for them, and re-layouts  2.67 us (3%)
    pallas_call x1, Pallas kernels, per_device(): pl.pallas_call(functools.partial(kernel, (n_gz, n_xy, width, (smag_coeff...  96 us
    unnamed x1, local copies, waits for them, and re-layouts  2.67 us

profile of v3, /device:TPU:17, one launch (start us, length us, event | category | flops | bytes accessed | tf_op | source)
XLA Modules:
  0.0 98.7 jit_solution(10078375623087213234)
XLA Ops:
  0.0 96.0 %shard_map.64 = f32[3,256,512]{2,1,0:T(8,128)} custom-call(f32[3,256,512]{2,1,0:T(8,128)} %bitcast.6, s32[1,128]{1,0:T(1,128)} %bitcast.7, f32[1,128]{1,0:T(1,128)} %constant.8.clone.weight_ref, bf16[4,256,256]{2,1,0:T(8,128)(2,1)} %constant.9.clone.mx_ref, bf16[576,256]{1,0:T(8,128)(2,1)} %constant.10.clone.my_ref, ...), custom_call_target="tpu_custom_call" | custom-call | tf_op jit(solution)/shard_map/pallas_call | solution.py:444
  96.0 2.7 %copy.9 = f32[1,3,1,256,512]{4,3,2,1,0:T(8,128)} copy(f32[1,3,1,256,512]{4,3,2,1,0:T(8,128)} %bitcast.5) | data formatting | bytes 3145728

commit v4 on v2

--- a/solution.py
+++ b/solution.py
@@ -11,9 +11,10 @@
 from jax.sharding import PartitionSpec as P
 
 STEPS = 2
-CHUNKS = 4
-ROWS = 8
-BLOCK = 256
+CHUNKS = 8
+PARTS = 2
+ROWS = 16
+BLOCK = 128
 
 time_step = 0.001
 level_gap = 0.05
@@ -72,6 +73,7 @@
     _, rows_all, cols_all = in_ref.shape
     half = cols_all // 2
     chunk = rows_all // CHUNKS
+    step = min(ROWS, chunk)
     grp, gz, xy = lax.axis_index("grp"), lax.axis_index("gz"), lax.axis_index("xy")
     domain = lax.rem(gz, 2)
     pair = gz - domain
@@ -95,41 +97,33 @@
     def xy_to(offset):
         return (grp, gz, lax.rem(xy + offset, n_xy))
 
-    bases = {}
-
-    def copy(name, index, source, target, device):
-        slot = bases.setdefault(name, len(bases) * 3 * CHUNKS) + index
+    slots = {}
+
+    def copy(name, source, target, device):
+        slot = slots.setdefault(name, len(slots))
         return pltpu.make_async_remote_copy(
             src_ref=source, dst_ref=target, send_sem=send_sem.at[slot],
             recv_sem=recv_sem.at[slot], device_id=device, device_id_type=MESH,
         )
 
-    def when(condition, action):
+    chunks = list(range(CHUNKS))
+    parts = [(c, part) for c in range(3) for part in range(PARTS)]
+
+    def region(ref, k):
+        if isinstance(k, tuple):
+            lines = rows_all // PARTS
+            return ref.at[k[0], pl.ds(k[1] * lines, lines), :]
+        return ref.at[:, pl.ds(k * chunk, chunk), :]
+
+    def flush(condition, copies):
+        def wait():
+            for item in copies:
+                item.wait_send()
+
         if condition is None:
-            action()
+            wait()
         else:
-            pl.when(condition)(action)
-
-    def part(ref, k):
-        return ref.at[pl.ds(k * chunk, chunk), :]
-
-    def each(body):
-        def step(c, carry):
-            body(c)
-            return carry
-
-        lax.fori_loop(0, 3, step, 0)
-
-    def flush(*waits):
-        def body(c):
-            for condition, copies in waits:
-                def wait():
-                    for item in copies(c):
-                        item.wait_send()
-
-                when(condition, wait)
-
-        each(body)
+            pl.when(condition)(wait)
 
     barrier = pltpu.get_barrier_semaphore()
     for device in [up, down, mid_to, end_to] + [xy_to(o) for o in range(1, n_xy)]:
@@ -144,51 +138,47 @@
     def _():
         pl.semaphore_wait(barrier, 3 + n_xy)
 
-    def z_copy(kind, s, c, k, upward):
+    def z_pieces(kind, s):
+        return parts if kind == "v" and s == 0 else chunks
+
+    def z_copy(kind, s, k, upward):
         source, halo = (vel, vhalo) if kind == "v" else (sz, shalo)
         side, device = (0, up) if upward else (1, down)
-        return copy(
-            (kind, s, side), c * CHUNKS + k, part(source.at[s, c], k), part(halo.at[s, side, c], k), device
-        )
-
-    def z_start(kind, s, c, k):
-        pl.when(has_up)(z_copy(kind, s, c, k, True).start)
-        pl.when(has_down)(z_copy(kind, s, c, k, False).start)
-
-    def z_wait(kind, s, components, k):
+        return copy((kind, s, side, k), region(source.at[s], k), region(halo.at[s, side], k), device)
+
+    def z_start(kind, s, k):
+        pl.when(has_up)(z_copy(kind, s, k, True).start)
+        pl.when(has_down)(z_copy(kind, s, k, False).start)
+
+    def z_wait(kind, s, pieces):
         def wait(upward):
-            for c in components:
-                z_copy(kind, s, c, k, upward).wait_recv()
+            for k in pieces:
+                z_copy(kind, s, k, upward).wait_recv()
 
         pl.when(has_down)(lambda: wait(True))
         pl.when(has_up)(lambda: wait(False))
 
     def z_flush(kind, s):
-        return [
-            (has_up, lambda c: [z_copy(kind, s, c, k, True) for k in range(CHUNKS)]),
-            (has_down, lambda c: [z_copy(kind, s, c, k, False) for k in range(CHUNKS)]),
-        ]
-
-    def swap_in(c, k):
-        return copy("in", c * CHUNKS + k, part(in_ref.at[c], k), part(vel.at[0, c], k), swap_to)
-
-    def swap_back(c, k):
-        return copy("out", c * CHUNKS + k, part(ret.at[c], k), part(fin.at[c], k), swap_to)
-
-    def fringe_copy(s, c, k):
+        flush(has_up, [z_copy(kind, s, k, True) for k in z_pieces(kind, s)])
+        flush(has_down, [z_copy(kind, s, k, False) for k in z_pieces(kind, s)])
+
+    def swap_in(k):
+        return copy(("in", k), region(in_ref, k), region(vel.at[0], k), swap_to)
+
+    def swap_back(k):
+        return copy(("out", k), region(ret, k), region(fin, k), swap_to)
+
+    def fringe_copy(s, k):
         device = end_to if s == STEPS - 1 else mid_to
-        return copy(("f", s), c * CHUNKS + k, part(psend.at[s, c], k), part(precv.at[s, c], k), device)
+        return copy(("f", s, k), region(psend.at[s], k), region(precv.at[s], k), device)
 
     def g_copy(index, o, c):
-        return copy(("g", index, o), c, gsend.at[index, c], grecv.at[index, o - 1, c], xy_to(o))
+        return copy(("g", index, o, c), gsend.at[index, c], grecv.at[index, o - 1, c], xy_to(o))
 
     @pl.when(swapped)
     def _():
-        def body(c):
-            for k in range(CHUNKS):
-                swap_in(c, k).start()
-
-        each(body)
+        for k in parts:
+            swap_in(k).start()
 
     @pl.when(jnp.logical_not(swapped))
     def _():
@@ -216,7 +206,8 @@
         middle = rest.astype(jnp.bfloat16)
         low = (rest - middle.astype(jnp.float32)).astype(jnp.bfloat16)
         wide = dot(jnp.concatenate([high, middle, low], axis=0), picker)
-        return (wide[:chunk] + (wide[chunk : 2 * chunk] + wide[2 * chunk :])) * weight_ref[...]
+        lines = field.shape[0]
+        return (wide[:lines] + (wide[lines : 2 * lines] + wide[2 * lines :])) * weight_ref[...]
 
     def x_derived(field):
         left, right = field[:, :half], field[:, half:]
@@ -247,7 +238,7 @@
         return result
 
     def g_flush(index):
-        return (None, lambda c: [g_copy(index, o, c) for o in range(1, n_xy)])
+        flush(None, [g_copy(index, o, c) for o in range(1, n_xy) for c in range(3)])
 
     def derive(s, c):
         field = vel[s, c]
@@ -256,26 +247,25 @@
 
     z_scale = 1.0 / (2.0 * level_gap)
 
-    def arrive(c):
-        for k in range(CHUNKS):
-            pl.when(swapped)(swap_in(c, k).wait_recv)
-            z_start("v", 0, c, k)
+    for c in range(3):
+        for k in parts:
+            if k[0] == c:
+                pl.when(swapped)(swap_in(k).wait_recv)
+                z_start("v", 0, k)
         derive(0, c)
-
-    each(arrive)
 
     for s in range(STEPS):
         last = s == STEPS - 1
-
-        def second(c):
-            if n_xy > 1:
+        if s > 0:
+            for c in range(3):
+                derive(s, c)
+        if n_xy > 1:
+            for c in range(3):
                 gy[c] = gy[c] + received(2 * s, c)
-
-        each(second)
 
         def pointwise(i, carry):
             for first in range(0, cols_all, BLOCK):
-                block(pl.ds(pl.multiple_of(i * ROWS, ROWS), ROWS), pl.ds(first, BLOCK))
+                block(pl.ds(pl.multiple_of(i * step, step), step), pl.ds(first, BLOCK))
             return carry
 
         def block(rows, lanes):
@@ -300,102 +290,84 @@
             sz[s, 1, rows, lanes] = yz
             sz[s, 2, rows, lanes] = eddy * zz
 
-        for k in range(CHUNKS):
-            z_wait("v", s, range(3), k)
-            lax.fori_loop(k * chunk // ROWS, (k + 1) * chunk // ROWS, pointwise, 0)
-            z_start("s", s, 0, k)
-        for c in (1, 2):
-            for k in range(CHUNKS):
-                z_start("s", s, c, k)
-
-        def third(c):
+        for k in chunks:
+            if s > 0:
+                z_wait("v", s, [k])
+            elif k % (CHUNKS // PARTS) == 0:
+                z_wait("v", s, [piece for piece in parts if piece[1] == k // (CHUNKS // PARTS)])
+            lax.fori_loop(k * chunk // step, (k + 1) * chunk // step, pointwise, 0)
+            z_start("s", s, k)
+
+        for c in range(3):
             tend[c] = tend[c] + y_derived(2 * s + 1, c, sy[c])
             tend[c] = tend[c] + x_derived(sx[c])
-
-        each(third)
-
-        def fourth(c):
-            if n_xy > 1:
+        if n_xy > 1:
+            for c in range(3):
                 tend[c] = tend[c] + received(2 * s + 1, c)
-
-        each(fourth)
-        flush(*z_flush("v", s), g_flush(2 * s), g_flush(2 * s + 1))
-
-        def update(c, k, target):
-            z_wait("s", s, [c], k)
+        z_flush("v", s)
+        g_flush(2 * s)
+        g_flush(2 * s + 1)
+
+        def update(k, target):
             rows = pl.ds(k * chunk, chunk)
-            along_z = (shalo[s, 1, c, rows, :] - shalo[s, 0, c, rows, :]) * z_scale
-            target[c, rows, :] = vel[s, c, rows, :] + time_step * (tend[c, rows, :] + along_z)
-
-        def pick(c, k, source):
+            for c in range(3):
+                along_z = (shalo[s, 1, c, rows, :] - shalo[s, 0, c, rows, :]) * z_scale
+                target[c, rows, :] = vel[s, c, rows, :] + time_step * (tend[c, rows, :] + along_z)
+
+        def pick(k, source):
             rows = pl.ds(k * chunk, chunk)
-            psend[s, c, rows, :] = picked(source[c, rows, :])
-            fringe_copy(s, c, k).start()
-
-        def blend(c, k, source, target):
-            fringe_copy(s, c, k).wait_recv()
+            fields = jnp.concatenate([source[c, rows, :] for c in range(3)], axis=0)
+            values = picked(fields)
+            for c in range(3):
+                psend[s, c, rows, :] = values[c * chunk : (c + 1) * chunk]
+            fringe_copy(s, k).start()
+
+        def blend(k, source, target):
+            fringe_copy(s, k).wait_recv()
             rows = pl.ds(k * chunk, chunk)
-            own = source[c, rows, :width] * (1.0 - weight_ref[...])
-            target[c, rows, :width] = own + precv[s, c, rows, :]
+            for c in range(3):
+                own = source[c, rows, :width] * (1.0 - weight_ref[...])
+                target[c, rows, :width] = own + precv[s, c, rows, :]
 
         if not last:
             following = vel.at[s + 1]
-
-            def advance(c):
-                for k in range(CHUNKS):
-                    update(c, k, following)
-
-                    @pl.when(jnp.logical_not(is_farm))
-                    def _():
-                        pick(c, k, following)
-                        z_start("v", s + 1, c, k)
-
-                @pl.when(is_farm)
+            for k in chunks:
+                z_wait("s", s, [k])
+                update(k, following)
+
+                @pl.when(jnp.logical_not(is_farm))
                 def _():
-                    for k in range(CHUNKS):
-                        blend(c, k, following, following)
-                        z_start("v", s + 1, c, k)
-
-                derive(s + 1, c)
-
-            each(advance)
-            flush(*z_flush("s", s))
+                    pick(k, following)
+
+                pl.when(is_farm)(lambda: blend(k, following, following))
+                z_start("v", s + 1, k)
+            z_flush("s", s)
+            flush(jnp.logical_not(is_farm), [fringe_copy(s, k) for k in chunks])
         else:
-            def finish(c):
-                for k in range(CHUNKS):
-                    pl.when(swapped)(swap_back(c, k).wait_recv)
-                    pl.when(grp == 1)(lambda: pick(c, k, fin))
-                    rows = pl.ds(k * chunk, chunk)
-                    out_ref[c, rows, :] = fin[c, rows, :]
-
-                @pl.when(grp == 0)
+            def finish(k):
+                pl.when(swapped)(swap_back(k).wait_recv)
+                pl.when(grp == 1)(lambda: pick(k, fin))
+                rows = pl.ds(k * chunk, chunk)
+                out_ref[:, rows, :] = fin[:, rows, :]
+                pl.when(grp == 0)(lambda: blend(k, fin, out_ref))
+
+            for k in chunks:
+                z_wait("s", s, [k])
+
+                @pl.when(swapped)
                 def _():
-                    for k in range(CHUNKS):
-                        blend(c, k, fin, out_ref)
-
-            def advance(c):
-                for k in range(CHUNKS):
-                    @pl.when(swapped)
-                    def _():
-                        update(c, k, ret)
-                        swap_back(c, k).start()
-
-                    pl.when(jnp.logical_not(swapped))(lambda: update(c, k, fin))
-
-                pl.when(c > 0)(lambda: finish(c - 1))
-
-            each(advance)
-            finish(2)
-            flush(
-                *z_flush("s", s),
-                (swapped, lambda c: [swap_in(c, k) for k in range(CHUNKS)]),
-                (swapped, lambda c: [swap_back(c, k) for k in range(CHUNKS)]),
-                (grp == 1, lambda c: [fringe_copy(s, c, k) for k in range(CHUNKS)]),
-                *[
-                    (jnp.logical_not(is_farm), lambda c, t=t: [fringe_copy(t, c, k) for k in range(CHUNKS)])
-                    for t in range(STEPS - 1)
-                ],
-            )
+                    update(k, ret)
+                    swap_back(k).start()
+
+                pl.when(jnp.logical_not(swapped))(lambda: update(k, fin))
+                if k == 1:
+                    flush(swapped, [swap_in(piece) for piece in parts])
+                if k > 0:
+                    finish(k - 1)
+            finish(CHUNKS - 1)
+            z_flush("s", s)
+            flush(swapped, [swap_back(k) for k in chunks])
+            flush(grp == 1, [fringe_copy(s, k) for k in chunks])
 
 
 def per_device(velocity, fringe_columns):
@@ -422,7 +394,7 @@
     weights = (0.5 * (1.0 + np.cos(np.pi * offsets / width))).astype(np.float32)[None]
     plane = (comps, rows_all, cols_all)
     fringe = (comps, rows_all, width)
-    copies = 3 * CHUNKS * (STEPS * 5 + 2 + 2 * STEPS * others)
+    copies = STEPS * (5 * CHUNKS + 6 * others) + CHUNKS + 9 * PARTS
     vmem = pl.BlockSpec(memory_space=pltpu.VMEM)
 
     def buffer(*shape):

time: 94.4 us -> 95.7 us (1.014)
  Pallas kernels: 90.3 us -> 91.6 us
    pallas_call x1, Pallas kernels: 90.3 us -> 91.6 us  [per_device(): pl.pallas_call(functools.partial(kernel, (n_gz, n_xy, width, (smag_coeff...]
where the time goes in v4:
time: 95.7 us; the launch traced here: 94.3 us
  Pallas kernels  91.6 us (96%)
  local copies, waits for them, and re-layouts  2.67 us (3%)
    pallas_call x1, Pallas kernels, per_device(): pl.pallas_call(functools.partial(kernel, (n_gz, n_xy, width, (smag_coeff...  91.6 us
    unnamed x1, local copies, waits for them, and re-layouts  2.67 us

profile of v4, /device:TPU:17, one launch (start us, length us, event | category | flops | bytes accessed | tf_op | source)
XLA Modules:
  0.0 94.3 jit_solution(17326845169293554173)
XLA Ops:
  0.0 91.6 %shard_map.64 = f32[3,256,512]{2,1,0:T(8,128)} custom-call(f32[3,256,512]{2,1,0:T(8,128)} %bitcast.6, s32[1,128]{1,0:T(1,128)} %bitcast.7, f32[1,128]{1,0:T(1,128)} %constant.8.clone.weight_ref, bf16[4,256,256]{2,1,0:T(8,128)(2,1)} %constant.9.clone.mx_ref, bf16[576,256]{1,0:T(8,128)(2,1)} %constant.10.clone.my_ref, ...), custom_call_target="tpu_custom_call" | custom-call | tf_op jit(solution)/shard_map/pallas_call | solution.py:403
  91.6 2.7 %copy.9 = f32[1,3,1,256,512]{4,3,2,1,0:T(8,128)} copy(f32[1,3,1,256,512]{4,3,2,1,0:T(8,128)} %bitcast.5) | data formatting | bytes 3145728

commit v5 on v4

--- a/solution.py
+++ b/solution.py
@@ -11,8 +11,7 @@
 from jax.sharding import PartitionSpec as P
 
 STEPS = 2
-CHUNKS = 8
-PARTS = 2
+CHUNKS = 4
 ROWS = 16
 BLOCK = 128
 
@@ -107,12 +106,8 @@
         )
 
     chunks = list(range(CHUNKS))
-    parts = [(c, part) for c in range(3) for part in range(PARTS)]
 
     def region(ref, k):
-        if isinstance(k, tuple):
-            lines = rows_all // PARTS
-            return ref.at[k[0], pl.ds(k[1] * lines, lines), :]
         return ref.at[:, pl.ds(k * chunk, chunk), :]
 
     def flush(condition, copies):
@@ -138,17 +133,16 @@
     def _():
         pl.semaphore_wait(barrier, 3 + n_xy)
 
-    def z_pieces(kind, s):
-        return parts if kind == "v" and s == 0 else chunks
-
     def z_copy(kind, s, k, upward):
         source, halo = (vel, vhalo) if kind == "v" else (sz, shalo)
         side, device = (0, up) if upward else (1, down)
         return copy((kind, s, side, k), region(source.at[s], k), region(halo.at[s, side], k), device)
 
     def z_start(kind, s, k):
-        pl.when(has_up)(z_copy(kind, s, k, True).start)
-        pl.when(has_down)(z_copy(kind, s, k, False).start)
+        upward, downward = z_copy(kind, s, k, True), z_copy(kind, s, k, False)
+        pl.when(jnp.logical_and(has_up, grp == 1))(upward.start)
+        pl.when(has_down)(downward.start)
+        pl.when(jnp.logical_and(has_up, grp == 0))(upward.start)
 
     def z_wait(kind, s, pieces):
         def wait(upward):
@@ -159,8 +153,8 @@
         pl.when(has_up)(lambda: wait(False))
 
     def z_flush(kind, s):
-        flush(has_up, [z_copy(kind, s, k, True) for k in z_pieces(kind, s)])
-        flush(has_down, [z_copy(kind, s, k, False) for k in z_pieces(kind, s)])
+        flush(has_up, [z_copy(kind, s, k, True) for k in chunks])
+        flush(has_down, [z_copy(kind, s, k, False) for k in chunks])
 
     def swap_in(k):
         return copy(("in", k), region(in_ref, k), region(vel.at[0], k), swap_to)
@@ -177,7 +171,7 @@
 
     @pl.when(swapped)
     def _():
-        for k in parts:
+        for k in chunks:
             swap_in(k).start()
 
     @pl.when(jnp.logical_not(swapped))
@@ -247,18 +241,14 @@
 
     z_scale = 1.0 / (2.0 * level_gap)
 
-    for c in range(3):
-        for k in parts:
-            if k[0] == c:
-                pl.when(swapped)(swap_in(k).wait_recv)
-                z_start("v", 0, k)
-        derive(0, c)
+    for k in chunks:
+        pl.when(swapped)(swap_in(k).wait_recv)
+        z_start("v", 0, k)
 
     for s in range(STEPS):
         last = s == STEPS - 1
-        if s > 0:
-            for c in range(3):
-                derive(s, c)
+        for c in range(3):
+            derive(s, c)
         if n_xy > 1:
             for c in range(3):
                 gy[c] = gy[c] + received(2 * s, c)
@@ -291,10 +281,7 @@
             sz[s, 2, rows, lanes] = eddy * zz
 
         for k in chunks:
-            if s > 0:
-                z_wait("v", s, [k])
-            elif k % (CHUNKS // PARTS) == 0:
-                z_wait("v", s, [piece for piece in parts if piece[1] == k // (CHUNKS // PARTS)])
+            z_wait("v", s, [k])
             lax.fori_loop(k * chunk // step, (k + 1) * chunk // step, pointwise, 0)
             z_start("s", s, k)
 
@@ -361,7 +348,7 @@
 
                 pl.when(jnp.logical_not(swapped))(lambda: update(k, fin))
                 if k == 1:
-                    flush(swapped, [swap_in(piece) for piece in parts])
+                    flush(swapped, [swap_in(piece) for piece in chunks])
                 if k > 0:
                     finish(k - 1)
             finish(CHUNKS - 1)
@@ -394,7 +381,7 @@
     weights = (0.5 * (1.0 + np.cos(np.pi * offsets / width))).astype(np.float32)[None]
     plane = (comps, rows_all, cols_all)
     fringe = (comps, rows_all, width)
-    copies = STEPS * (5 * CHUNKS + 6 * others) + CHUNKS + 9 * PARTS
+    copies = STEPS * (5 * CHUNKS + 6 * others) + 2 * CHUNKS
     vmem = pl.BlockSpec(memory_space=pltpu.VMEM)
 
     def buffer(*shape):

time: 95.7 us -> 93.3 us (0.975)
  Pallas kernels: 91.6 us -> 89.9 us
    pallas_call x1, Pallas kernels: 91.6 us -> 89.9 us  [per_device(): pl.pallas_call(functools.partial(kernel, (n_gz, n_xy, width, (smag_coeff...]
where the time goes in v5:
time: 93.3 us; the launch traced here: 92.5 us
  Pallas kernels  89.9 us (96%)
  local copies, waits for them, and re-layouts  2.67 us (3%)
    pallas_call x1, Pallas kernels, per_device(): pl.pallas_call(functools.partial(kernel, (n_gz, n_xy, width, (smag_coeff...  89.9 us
    unnamed x1, local copies, waits for them, and re-layouts  2.67 us

profile of v5, /device:TPU:17, one launch (start us, length us, event | category | flops | bytes accessed | tf_op | source)
XLA Modules:
  0.0 92.5 jit_solution(14727255171641869403)
XLA Ops:
  0.0 89.9 %shard_map.64 = f32[3,256,512]{2,1,0:T(8,128)} custom-call(f32[3,256,512]{2,1,0:T(8,128)} %bitcast.6, s32[1,128]{1,0:T(1,128)} %bitcast.7, f32[1,128]{1,0:T(1,128)} %constant.8.clone.weight_ref, bf16[4,256,256]{2,1,0:T(8,128)(2,1)} %constant.9.clone.mx_ref, bf16[576,256]{1,0:T(8,128)(2,1)} %constant.10.clone.my_ref, ...), custom_call_target="tpu_custom_call" | custom-call | tf_op jit(solution)/shard_map/pallas_call | solution.py:390
  89.9 2.7 %copy.9 = f32[1,3,1,256,512]{4,3,2,1,0:T(8,128)} copy(f32[1,3,1,256,512]{4,3,2,1,0:T(8,128)} %bitcast.5) | data formatting | bytes 3145728

commit v6 on v5

--- a/solution.py
+++ b/solution.py
@@ -92,6 +92,7 @@
     swap_to = (domain, pair + grp, xy)
     mid_to = (grp, pair + 1 - domain, xy)
     end_to = (1 - grp, gz, xy)
+    farm_to = (0, pair + grp, xy)
 
     def xy_to(offset):
         return (grp, gz, lax.rem(xy + offset, n_xy))
@@ -107,8 +108,14 @@
 
     chunks = list(range(CHUNKS))
 
-    def region(ref, k):
-        return ref.at[:, pl.ds(k * chunk, chunk), :]
+    def region(ref, k, lanes=None):
+        first, count = lanes or (0, ref.shape[-1])
+        return ref.at[:, pl.ds(k * chunk, chunk), pl.ds(first, count)]
+
+    def spans(kind, s):
+        if kind == "v" and s > 0:
+            return [(width, cols_all - width), (0, width)]
+        return [(0, cols_all)]
 
     def flush(condition, copies):
         def wait():
@@ -133,28 +140,32 @@
     def _():
         pl.semaphore_wait(barrier, 3 + n_xy)
 
-    def z_copy(kind, s, k, upward):
+    def z_copy(kind, s, k, upward, lanes):
         source, halo = (vel, vhalo) if kind == "v" else (sz, shalo)
         side, device = (0, up) if upward else (1, down)
-        return copy((kind, s, side, k), region(source.at[s], k), region(halo.at[s, side], k), device)
-
-    def z_start(kind, s, k):
-        upward, downward = z_copy(kind, s, k, True), z_copy(kind, s, k, False)
+        return copy(
+            (kind, s, side, k, lanes),
+            region(source.at[s], k, lanes), region(halo.at[s, side], k, lanes), device,
+        )
+
+    def z_start(kind, s, k, lanes=None):
+        lanes = lanes or (0, cols_all)
+        upward, downward = z_copy(kind, s, k, True, lanes), z_copy(kind, s, k, False, lanes)
         pl.when(jnp.logical_and(has_up, grp == 1))(upward.start)
         pl.when(has_down)(downward.start)
         pl.when(jnp.logical_and(has_up, grp == 0))(upward.start)
 
-    def z_wait(kind, s, pieces):
+    def z_wait(kind, s, k):
         def wait(upward):
-            for k in pieces:
-                z_copy(kind, s, k, upward).wait_recv()
+            for lanes in spans(kind, s):
+                z_copy(kind, s, k, upward, lanes).wait_recv()
 
         pl.when(has_down)(lambda: wait(True))
         pl.when(has_up)(lambda: wait(False))
 
     def z_flush(kind, s):
-        flush(has_up, [z_copy(kind, s, k, True) for k in chunks])
-        flush(has_down, [z_copy(kind, s, k, False) for k in chunks])
+        for condition, upward in ((has_up, True), (has_down, False)):
+            flush(condition, [z_copy(kind, s, k, upward, lanes) for k in chunks for lanes in spans(kind, s)])
 
     def swap_in(k):
         return copy(("in", k), region(in_ref, k), region(vel.at[0], k), swap_to)
@@ -163,7 +174,7 @@
         return copy(("out", k), region(ret, k), region(fin, k), swap_to)
 
     def fringe_copy(s, k):
-        device = end_to if s == STEPS - 1 else mid_to
+        device = farm_to if s == STEPS - 1 else mid_to
         return copy(("f", s, k), region(psend.at[s], k), region(precv.at[s], k), device)
 
     def g_copy(index, o, c):
@@ -281,7 +292,7 @@
             sz[s, 2, rows, lanes] = eddy * zz
 
         for k in chunks:
-            z_wait("v", s, [k])
+            z_wait("v", s, k)
             lax.fori_loop(k * chunk // step, (k + 1) * chunk // step, pointwise, 0)
             z_start("s", s, k)
 
@@ -318,43 +329,50 @@
 
         if not last:
             following = vel.at[s + 1]
+            beyond, within = spans("v", s + 1)
             for k in chunks:
-                z_wait("s", s, [k])
+                z_wait("s", s, k)
                 update(k, following)
+                z_start("v", s + 1, k, beyond)
 
                 @pl.when(jnp.logical_not(is_farm))
                 def _():
                     pick(k, following)
-
-                pl.when(is_farm)(lambda: blend(k, following, following))
-                z_start("v", s + 1, k)
+                    z_start("v", s + 1, k, within)
+
+            @pl.when(is_farm)
+            def _():
+                for k in chunks:
+                    blend(k, following, following)
+                    z_start("v", s + 1, k, within)
+
             z_flush("s", s)
             flush(jnp.logical_not(is_farm), [fringe_copy(s, k) for k in chunks])
         else:
             def finish(k):
                 pl.when(swapped)(swap_back(k).wait_recv)
-                pl.when(grp == 1)(lambda: pick(k, fin))
                 rows = pl.ds(k * chunk, chunk)
                 out_ref[:, rows, :] = fin[:, rows, :]
                 pl.when(grp == 0)(lambda: blend(k, fin, out_ref))
 
+            def advance(k, target):
+                update(k, target)
+                if target is ret:
+                    swap_back(k).start()
+                pl.when(jnp.logical_not(is_farm))(lambda: pick(k, target))
+
             for k in chunks:
-                z_wait("s", s, [k])
-
-                @pl.when(swapped)
-                def _():
-                    update(k, ret)
-                    swap_back(k).start()
-
-                pl.when(jnp.logical_not(swapped))(lambda: update(k, fin))
-                if k == 1:
-                    flush(swapped, [swap_in(piece) for piece in chunks])
-                if k > 0:
-                    finish(k - 1)
-            finish(CHUNKS - 1)
+                z_wait("s", s, k)
+                pl.when(swapped)(lambda: advance(k, ret))
+                pl.when(jnp.logical_not(swapped))(lambda: advance(k, fin))
+                if k > 1:
+                    finish(k - 2)
+            for k in chunks[-2:]:
+                finish(k)
+            flush(swapped, [swap_in(k) for k in chunks])
             z_flush("s", s)
             flush(swapped, [swap_back(k) for k in chunks])
-            flush(grp == 1, [fringe_copy(s, k) for k in chunks])
+            flush(jnp.logical_not(is_farm), [fringe_copy(s, k) for k in chunks])
 
 
 def per_device(velocity, fringe_columns):
@@ -381,7 +399,7 @@
     weights = (0.5 * (1.0 + np.cos(np.pi * offsets / width))).astype(np.float32)[None]
     plane = (comps, rows_all, cols_all)
     fringe = (comps, rows_all, width)
-    copies = STEPS * (5 * CHUNKS + 6 * others) + 2 * CHUNKS
+    copies = STEPS * (7 * CHUNKS + 6 * others) + 2 * CHUNKS
     vmem = pl.BlockSpec(memory_space=pltpu.VMEM)
 
     def buffer(*shape):

time: 93.3 us -> 92.8 us (level)
  the two profiles are of different devices: /device:TPU:17 before, /device:TPU:1 now
where the time goes in v6:
time: 92.8 us; the launch traced here: 92.7 us
  Pallas kernels  90 us (97%)
  local copies, waits for them, and re-layouts  2.67 us (3%)
    pallas_call x1, Pallas kernels, per_device(): pl.pallas_call(functools.partial(kernel, (n_gz, n_xy, width, (smag_coeff...  90 us
    unnamed x1, local copies, waits for them, and re-layouts  2.67 us

profile of v6, /device:TPU:1, one launch (start us, length us, event | category | flops | bytes accessed | tf_op | source)
XLA Modules:
  0.0 92.7 jit_solution(14168385181631215689)
XLA Ops:
  0.0 90.0 %shard_map.64 = f32[3,256,512]{2,1,0:T(8,128)} custom-call(f32[3,256,512]{2,1,0:T(8,128)} %bitcast.6, s32[1,128]{1,0:T(1,128)} %bitcast.7, f32[1,128]{1,0:T(1,128)} %constant.8.clone.weight_ref, bf16[4,256,256]{2,1,0:T(8,128)(2,1)} %constant.9.clone.mx_ref, bf16[576,256]{1,0:T(8,128)(2,1)} %constant.10.clone.my_ref, ...), custom_call_target="tpu_custom_call" | custom-call | tf_op jit(solution)/shard_map/pallas_call | solution.py:408
  90.0 2.7 %copy.9 = f32[1,3,1,256,512]{4,3,2,1,0:T(8,128)} copy(f32[1,3,1,256,512]{4,3,2,1,0:T(8,128)} %bitcast.5) | data formatting | bytes 3145728

commit v7 on v0

--- a/solution.py
+++ b/solution.py
@@ -67,7 +67,7 @@
 
 
 def kernel(
-    sizes, in_ref, cols_ref, weight_ref, mx_ref, my_ref, gather_ref, spread_ref, out_ref,
+    sizes, in_ref, cols_ref, weight_ref, mx_ref, my_ref, gather_ref, spread_ref, out_ref, picks_ref,
     vel, ret, fin, vhalo, shalo, gx, gy, tend, sx, sy, sz, gsend, grecv, psend, precv,
     send_sem, recv_sem,
 ):
@@ -352,7 +352,11 @@
                 @pl.when(grp == 0)
                 def _():
                     fringe_copy(k, end_to).wait_recv()
-                    blend(k, fin, out_ref)
+                    picks_ref[:, rows, :] = precv[s, :, rows, :]
+
+                @pl.when(grp == 1)
+                def _():
+                    picks_ref[:, rows, :] = jnp.zeros((3, chunk, width), jnp.float32)
 
     for condition, item in pending:
         if condition is None:
@@ -391,11 +395,11 @@
     def buffer(*shape):
         return pltpu.VMEM(shape, jnp.float32)
 
-    result = pl.pallas_call(
+    result, picks = pl.pallas_call(
         functools.partial(kernel, (n_gz, n_xy, width, (smag_coeff * delta) ** 2)),
-        out_shape=jax.ShapeDtypeStruct(plane, jnp.float32),
+        out_shape=[jax.ShapeDtypeStruct(plane, jnp.float32), jax.ShapeDtypeStruct(fringe, jnp.float32)],
         in_specs=[vmem] * 7,
-        out_specs=vmem,
+        out_specs=[vmem, vmem],
         scratch_shapes=[
             buffer(STEPS, *plane),
             buffer(*plane),
@@ -422,7 +426,10 @@
         velocity.reshape(plane), fringe_columns.reshape(1, width), jnp.asarray(weights),
         jnp.asarray(mx), jnp.asarray(my), jnp.asarray(gather), jnp.asarray(spread),
     )
-    return result.reshape(velocity.shape)
+    kept = jnp.where(lax.axis_index("grp") == 0, 1.0 - jnp.asarray(weights), 1.0)
+    kept = jnp.pad(kept, ((0, 0), (0, cols_all - width)), constant_values=1.0)
+    added = jnp.pad(picks, ((0, 0), (0, 0), (0, cols_all - width)))
+    return (result * kept + added).reshape(velocity.shape)
 
 
 def solution(mesh):

time: 91.7 us -> 92.7 us (1.011)
  other arithmetic: 0 us -> 2.92 us
  local copies, waits for them, and re-layouts: 2.67 us -> 0.01 us
    reshape x0 -> x1, other arithmetic: none -> 2.91 us  [per_device(): return (result * kept + added).reshape(velocity.shape)]
    unnamed x1 -> x0, local copies, waits for them, and re-layouts: 2.67 us -> none
where the time goes in v7:
time: 92.7 us; the launch traced here: 91.4 us
  Pallas kernels  88.5 us (95%)
  other arithmetic  2.92 us (3%)
    pallas_call x1, Pallas kernels, per_device(): pl.pallas_call(functools.partial(kernel, (n_gz, n_xy, width, (smag_coeff...  88.5 us
    reshape x1, other arithmetic, per_device(): return (result * kept + added).reshape(velocity.shape)  2.91 us

profile of v7, /device:TPU:17, one launch (start us, length us, event | category | flops | bytes accessed | tf_op | source)
XLA Modules:
  0.0 91.4 jit_solution(4672483186233775754)
XLA Ops:
  0.0 88.5 %shard_map.73 = (f32[3,256,512]{2,1,0:T(8,128)}, f32[3,256,128]{2,1,0:T(8,128)}) custom-call(f32[3,256,512]{2,1,0:T(8,128)} %bitcast.7, s32[1,128]{1,0:T(1,128)} %bitcast.9, f32[1,128]{1,0:T(1,128)} %constant.23.clone.weight_ref, bf16[4,256,256]{2,1,0:T(8,128)(2,1)} %constant.24.clone.mx_ref, bf16[2,256,256]{2,1,0:T(8,128)(2,1)} %constant.25.clone.my_ref, ...), custom_call_target="tpu_custom_call" | custom-call | tf_op jit(solution)/shard_map/pallas_call | solution.py:398
  88.5 2.9 %add_bitcast_fusion = f32[1,3,1,256,512]{4,3,2,1,0:T(8,128)} fusion(f32[3,256,128]{2,1,0:T(8,128)} %get-tuple-element.8, f32[3,256,512]{2,1,0:T(8,128)} %get-tuple-element.7, f32[512]{0:T(512)S(1)} %bitcast.8), kind=kLoop, calls=%fused_computation | loop fusion | flops 786432 | bytes 3540992 | tf_op jit(solution)/shard_map/reshape | solution.py:432
  (2 shorter events, 0.0 us)

commit v8 on v0

--- a/solution.py
+++ b/solution.py
@@ -141,8 +141,10 @@
 
     def z_start(kind, s, k):
         upward, downward = z_copies(kind, s, k)
-        start(has_up, upward)
-        start(has_down, downward)
+        pending.extend([(has_up, upward), (has_down, downward)])
+        pl.when(jnp.logical_and(has_up, grp == 1))(upward.start)
+        pl.when(has_down)(downward.start)
+        pl.when(jnp.logical_and(has_up, grp == 0))(upward.start)
 
     def z_wait(kind, s, k):
         upward, downward = z_copies(kind, s, k)

time: 91.7 us -> 91.7 us (level)
  no operation moved by 1% of the time
where the time goes in v8:
time: 91.7 us; the launch traced here: 90.4 us
  Pallas kernels  87.7 us (96%)
  local copies, waits for them, and re-layouts  2.67 us (3%)
    pallas_call x1, Pallas kernels, per_device(): pl.pallas_call(functools.partial(kernel, (n_gz, n_xy, width, (smag_coeff...  87.7 us
    unnamed x1, local copies, waits for them, and re-layouts  2.67 us

profile of v8, /device:TPU:17, one launch (start us, length us, event | category | flops | bytes accessed | tf_op | source)
XLA Modules:
  0.0 90.4 jit_solution(12088754455643806917)
XLA Ops:
  0.0 87.7 %shard_map.73 = f32[3,256,512]{2,1,0:T(8,128)} custom-call(f32[3,256,512]{2,1,0:T(8,128)} %bitcast.6, s32[1,128]{1,0:T(1,128)} %bitcast.7, f32[1,128]{1,0:T(1,128)} %constant.10.clone.weight_ref, bf16[4,256,256]{2,1,0:T(8,128)(2,1)} %constant.11.clone.mx_ref, bf16[2,256,256]{2,1,0:T(8,128)(2,1)} %constant.12.clone.my_ref, ...), custom_call_target="tpu_custom_call" | custom-call | tf_op jit(solution)/shard_map/pallas_call | solution.py:396
  87.7 2.7 %copy.10 = f32[1,3,1,256,512]{4,3,2,1,0:T(8,128)} copy(f32[1,3,1,256,512]{4,3,2,1,0:T(8,128)} %bitcast.5) | data formatting | bytes 3145728
